TPU v7x, 256 devices: a whole 4x4x8 slice. The times are simulated.
256 devices in a mesh: front: 16 (over x, z_lo, core), row: 4 (over z_hi), col: 4 (over y).
Axes of the slice: x: 4, y: 4, z: 8 (z_hi: 4, z_lo: 2; z = z_hi * 2 + z_lo), core: 2. Of those that a mesh axis runs over, the one named last changes fastest.
Arguments:
- front_entries: float32 [65536, 4096], P(('front', 'row'), 'col'), parts along dimension 0, may hold values from -2 to 8, as said below
- child_updates: bfloat16 [65536, 2048], P(('front', 'row'), 'col'), parts along dimension 0, may hold values from -1 to 1, as said below
- child_maps: int32 [32, 16], P('front'), parts along dimension 0, may hold values from 0 to 31, as said below
Outputs:
- factored: float32 [65536, 4096], P(('front', 'row'), 'col'), parts along dimension 0
There are 16 independent parts, one for each index of `front`. A program takes and returns all parts, laid end to end along the dimension named above; each array names one. Nothing has to cross between parts.
Inputs may be any that keep to these rules, and one draw needn't show every extreme that they name: `front_entries`: symmetric; every diagonal entry of the rows from 1024 on lies in 3.5 to 7; the leading 1024 x 1024 block of the assembled front is positive definite. `child_updates`: each sibling's 2048 x 2048 block is symmetric. `child_maps`: each row lists 2048/128 distinct parent block numbers in decreasing order and contains every block number below 8.
All inputs are finite; a program needn't handle non-finite values.
Results may differ from a plain program's by a relative error of at most 0.0003.
Values may be sent and summed in bfloat16 or wider, within the bound.
A program may use at most 128 MiB of HBM per device.

v0:
```python
import jax
import jax.numpy as jnp
from jax import lax
from jax.sharding import PartitionSpec as P

P_SIZE = 1024
CU = 2048
B = 256
NB = 128
HIGHEST = lax.Precision.HIGHEST


def from_root(value, axis, root):
    mine = lax.axis_index(axis) == root
    return lax.psum(jnp.where(mine, value, jnp.zeros_like(value)), axis)


def block_select(parents, anchor, width):
    return parents[:, None] - anchor == jnp.arange(width, dtype=jnp.int32)[None, :]


def solve_panel(column_rows, diag_factor, global_rows, anchor):
    solved = jax.scipy.linalg.solve_triangular(diag_factor, column_rows.T, lower=True).T
    keeping = global_rows[:, None] >= anchor + jnp.arange(B, dtype=jnp.int32)[None, :]
    return jnp.where(keeping, solved, 0.0)


def local(front_entries, child_updates, child_maps):
    n_row = lax.axis_size("row")
    n_col = lax.axis_size("col")
    row_index = lax.axis_index("row")
    col_index = lax.axis_index("col")
    tile_rows, tile_cols = front_entries.shape
    row_blocks = tile_rows // NB
    col_blocks = tile_cols // NB
    child_blocks = CU // NB
    flat_maps = child_maps.reshape(-1)
    sibling = row_index // (n_row // 2)
    gather_portion = lax.all_gather(child_updates, "col", axis=1, tiled=True)
    block_count = gather_portion.shape[1] // NB
    parents = lax.dynamic_slice_in_dim(flat_maps, sibling * child_blocks, block_count)
    select = block_select(parents, col_index * col_blocks, col_blocks).astype(jnp.bfloat16)
    shaped = gather_portion.reshape(gather_portion.shape[0], block_count, NB)
    gather_placed = jnp.einsum("rjk,ji->rik", shaped, select, preferred_element_type=jnp.float32)
    regrouped = gather_placed.reshape(gather_portion.shape[0], tile_cols).astype(jnp.bfloat16)

    def gather_rows(running, portion):
        block_count = portion.shape[0] // NB
        select = block_select(flat_maps, row_index * row_blocks, row_blocks).astype(jnp.bfloat16)
        placed = lax.dot_general(
            select,
            portion.reshape(block_count, NB * tile_cols),
            (((0,), (0,)), ((), ())),
            preferred_element_type=jnp.float32,
        )
        return running + placed.reshape(tile_rows, tile_cols)

    assembled = gather_rows(front_entries, lax.all_gather(regrouped, "row", axis=0, tiled=True))
    panels = P_SIZE // B
    global_rows = row_index * tile_rows + jnp.arange(tile_rows, dtype=jnp.int32)
    global_cols = col_index * tile_cols + jnp.arange(tile_cols, dtype=jnp.int32)
    factor = jnp.zeros((tile_rows, tile_cols), jnp.float32)
    trailing = assembled
    for number in range(panels):
        anchor = number * B
        owner_col = anchor // tile_cols
        owner_row = anchor // tile_rows
        within = anchor % tile_cols
        within_row = anchor % tile_rows
        corner = trailing[within_row : within_row + B, within : within + B]
        corner = from_root(corner, ("row", "col"), owner_row * n_col + owner_col)
        diag_factor = jnp.linalg.cholesky(corner)
        column = from_root(trailing[:, within : within + B], "col", owner_col)
        share_rows = tile_rows // n_col
        portion = lax.dynamic_slice_in_dim(column, col_index * share_rows, share_rows, 0)
        portion_rows = (
            row_index * tile_rows + col_index * share_rows + jnp.arange(share_rows, dtype=jnp.int32)
        )
        solved = solve_panel(portion, diag_factor, portion_rows, anchor)
        complete = lax.all_gather(solved, ("row", "col"), axis=0, tiled=True)
        own_rows = lax.dynamic_slice_in_dim(complete, row_index * tile_rows, tile_rows, 0)
        col_rows = lax.dynamic_slice_in_dim(complete, col_index * tile_cols, tile_cols, 0)
        placed = lax.dynamic_update_slice(factor, own_rows, (0, within))
        factor = jnp.where(col_index == owner_col, placed, factor)
        update = lax.dot_general(
            own_rows,
            col_rows,
            (((1,), (1,)), ((), ())),
            precision=HIGHEST,
            preferred_element_type=jnp.float32,
        )
        trailing = jnp.where(global_cols[None, :] >= anchor + B, trailing - update, trailing)
    return jnp.where(
        global_cols[None, :] < P_SIZE,
        factor,
        jnp.where(global_rows[:, None] >= P_SIZE, trailing, 0.0),
    )


def solution(mesh):
    placed = (P(("front", "row"), "col"), P(("front", "row"), "col"), P("front", None))
    return jax.shard_map(
        local, mesh=mesh, in_specs=placed, out_specs=P(("front", "row"), "col"), check_vma=False
    )
```

profile of v0, /device:TPU:1, one launch (start us, length us, event | category | flops | bytes accessed | tf_op | source)
XLA Modules:
  0.0 1554.0 jit_solution(12450456545128269763)
XLA Ops:
  8.1 55.7 %all-gather.7.cloned.1.call-done = bf16[1024,2048]{1,0:T(8,128)(2,1)} async-done(((bf16[1024,512]{1,0:T(8,128)(2,1)}), bf16[1024,2048]{1,0:T(8,128)(2,1)}) %all-gather.7.cloned.1.call-update) | async-done | bytes 4194320 | tf_op jit(solution)/shard_map/all_gather | solution.py:39
  75.6 150.4 %all-gather.9.cloned.1.call-done = bf16[4096,1024]{1,0:T(8,128)(2,1)} async-done(((bf16[1024,1024]{1,0:T(8,128)(2,1)}), bf16[4096,1024]{1,0:T(8,128)(2,1)}) %all-gather.9.cloned.1.call-update) | async-done | bytes 8388624 | tf_op jit(solution)/shard_map/all_gather | solution.py:58
  225.9 8.9 reshape.84
  234.8 6.6 fusion.48
  261.7 150.5 %all-reduce.11.cloned.1.call-done = f32[256,256]{0,1:T(8,128)} async-done(((f32[256,256]{0,1:T(8,128)}), f32[256,256]{0,1:T(8,128)}) %all-reduce.11.cloned.1.call-update) | async-done | bytes 262160 | tf_op jit(solution)/shard_map/psum | solution.py:15
  414.2 11.7 cholesky.214
  426.0 9.8 custom-call.17
  436.3 11.7 cholesky.231
  454.5 19.7 %custom-call.18 = f32[2,128,128]{1,2,0:T(8,128)S(1)} custom-call(f32[2,128,128]{2,1,0:T(8,128)S(1)} %get-tuple-element.33), custom_call_target="InvertDiagBlocksLowerTriangular" | custom-call | tf_op jit(solution)/shard_map/jit(_solve_triangular)/triangular_solve | solution.py:23
  476.9 91.8 %all-gather.11.cloned.1.call-done = f32[4096,256]{0,1:T(8,128)} async-done(((f32[256,256]{0,1:T(8,128)}), f32[4096,256]{0,1:T(8,128)}) %all-gather.11.cloned.1.call-update) | async-done | bytes 4194320 | tf_op jit(solution)/shard_map/all_gather | solution.py:80
  570.0 8.3 subtract_select_fusion.3
  583.7 150.1 %all-reduce.15.cloned.1.call-done = f32[256,256]{0,1:T(8,128)} async-done(((f32[256,256]{0,1:T(8,128)}), f32[256,256]{0,1:T(8,128)}) %all-reduce.15.cloned.1.call-update) | async-done | bytes 262160 | tf_op jit(solution)/shard_map/psum | solution.py:15
  735.8 11.7 cholesky.248
  747.6 9.8 custom-call.19
  757.9 11.7 cholesky.265
  776.4 19.7 %custom-call.20 = f32[2,128,128]{1,2,0:T(8,128)S(1)} custom-call(f32[2,128,128]{2,1,0:T(8,128)S(1)} %get-tuple-element.34), custom_call_target="InvertDiagBlocksLowerTriangular" | custom-call | tf_op jit(solution)/shard_map/jit(_solve_triangular)/triangular_solve | solution.py:23
  798.8 91.8 %all-gather.13.cloned.1.call-done = f32[4096,256]{0,1:T(8,128)} async-done(((f32[256,256]{0,1:T(8,128)}), f32[4096,256]{0,1:T(8,128)}) %all-gather.13.cloned.1.call-update) | async-done | bytes 4194320 | tf_op jit(solution)/shard_map/all_gather | solution.py:80
  890.7 6.9 subtract_select_fusion.2
  903.1 149.9 %all-reduce.19.cloned.1.call-done = f32[256,256]{0,1:T(8,128)} async-done(((f32[256,256]{0,1:T(8,128)}), f32[256,256]{0,1:T(8,128)}) %all-reduce.19.cloned.1.call-update) | async-done | bytes 262160 | tf_op jit(solution)/shard_map/psum | solution.py:15
  1055.0 11.7 cholesky.282
  1066.8 9.8 custom-call.21
  1077.1 11.7 cholesky.299
  1095.7 19.7 %custom-call.22 = f32[2,128,128]{1,2,0:T(8,128)S(1)} custom-call(f32[2,128,128]{2,1,0:T(8,128)S(1)} %get-tuple-element.35), custom_call_target="InvertDiagBlocksLowerTriangular" | custom-call | tf_op jit(solution)/shard_map/jit(_solve_triangular)/triangular_solve | solution.py:23
  1118.2 91.8 %all-gather.15.cloned.1.call-done = f32[4096,256]{0,1:T(8,128)} async-done(((f32[256,256]{0,1:T(8,128)}), f32[4096,256]{0,1:T(8,128)}) %all-gather.15.cloned.1.call-update) | async-done | bytes 4194320 | tf_op jit(solution)/shard_map/all_gather | solution.py:80
  1210.0 6.9 subtract_select_fusion.1
  1222.3 150.1 %all-reduce.23.cloned.1.call-done = f32[256,256]{0,1:T(8,128)} async-done(((f32[256,256]{0,1:T(8,128)}), f32[256,256]{0,1:T(8,128)}) %all-reduce.23.cloned.1.call-update) | async-done | bytes 262160 | tf_op jit(solution)/shard_map/psum | solution.py:15
  1374.5 11.7 cholesky.316
  1386.3 9.8 custom-call.23
  1396.6 11.7 cholesky.333
  1414.7 19.7 %custom-call.24 = f32[2,128,128]{1,2,0:T(8,128)S(1)} custom-call(f32[2,128,128]{2,1,0:T(8,128)S(1)} %get-tuple-element.36), custom_call_target="InvertDiagBlocksLowerTriangular" | custom-call | tf_op jit(solution)/shard_map/jit(_solve_triangular)/triangular_solve | solution.py:23
  1445.0 84.0 %all-gather.17.cloned.1.call-done = f32[4096,256]{0,1:T(8,128)} async-done(((f32[256,256]{0,1:T(8,128)}), f32[4096,256]{0,1:T(8,128)}) %all-gather.17.cloned.1.call-update) | async-done | bytes 4194320 | tf_op jit(solution)/shard_map/all_gather | solution.py:80
  1531.7 10.2 fusion.1
  (170 shorter events, 124.7 us)
Async XLA Ops:
  6.5 57.3 %all-gather.7.cloned.1.call-start = ((), (), s32[]{:S(2)}) async-start(), calls=%async_computation | async-start | bytes 5242880 | tf_op jit(solution)/shard_map/all_gather | solution.py:39
  7.3 218.7 %all-gather.9.cloned.1.call-start = ((), (), s32[]{:S(2)}) async-start(), calls=%async_computation.1 | async-start | bytes 10485760 | tf_op jit(solution)/shard_map/all_gather | solution.py:58
  70.1 342.0 %all-reduce.11.cloned.1.call-start = ((), (), s32[]{:S(2)}) async-start(), calls=%async_computation.2 | async-start | bytes 524288 | tf_op jit(solution)/shard_map/psum | solution.py:15
  256.1 2.0 copy-start
  258.9 215.3 %all-reduce.13.cloned.1.call-start = ((), (), s32[]{:S(2)}) async-start(), calls=%async_computation.3 | async-start | bytes 2097152 | tf_op jit(solution)/shard_map/psum | solution.py:15
  261.3 307.4 %all-gather.11.cloned.1.call-start = ((), (), s32[]{:S(2)}) async-start(), calls=%async_computation.4 | async-start | bytes 4456448 | tf_op jit(solution)/shard_map/all_gather | solution.py:80
  476.8 256.9 %all-reduce.15.cloned.1.call-start = ((), (), s32[]{:S(2)}) async-start(), calls=%async_computation.5 | async-start | bytes 524288 | tf_op jit(solution)/shard_map/psum | solution.py:15
  578.3 2.0 copy-start.1
  581.0 215.0 %all-reduce.17.cloned.1.call-start = ((), (), s32[]{:S(2)}) async-start(), calls=%async_computation.6 | async-start | bytes 2097152 | tf_op jit(solution)/shard_map/psum | solution.py:15
  583.5 307.2 %all-gather.13.cloned.1.call-start = ((), (), s32[]{:S(2)}) async-start(), calls=%async_computation.7 | async-start | bytes 4456448 | tf_op jit(solution)/shard_map/all_gather | solution.py:80
  798.8 254.2 %all-reduce.19.cloned.1.call-start = ((), (), s32[]{:S(2)}) async-start(), calls=%async_computation.8 | async-start | bytes 524288 | tf_op jit(solution)/shard_map/psum | solution.py:15
  897.6 2.0 copy-start.2
  900.3 215.1 %all-reduce.21.cloned.1.call-start = ((), (), s32[]{:S(2)}) async-start(), calls=%async_computation.9 | async-start | bytes 2097152 | tf_op jit(solution)/shard_map/psum | solution.py:15
  902.8 307.3 %all-gather.15.cloned.1.call-start = ((), (), s32[]{:S(2)}) async-start(), calls=%async_computation.10 | async-start | bytes 4456448 | tf_op jit(solution)/shard_map/all_gather | solution.py:80
  1118.1 254.3 %all-reduce.23.cloned.1.call-start = ((), (), s32[]{:S(2)}) async-start(), calls=%async_computation.11 | async-start | bytes 524288 | tf_op jit(solution)/shard_map/psum | solution.py:15
  1217.0 2.0 copy-start.3
  1219.7 214.7 %all-reduce.25.cloned.1.call-start = ((), (), s32[]{:S(2)}) async-start(), calls=%async_computation.12 | async-start | bytes 2097152 | tf_op jit(solution)/shard_map/psum | solution.py:15
  1222.0 306.9 %all-gather.17.cloned.1.call-start = ((), (), s32[]{:S(2)}) async-start(), calls=%async_computation.13 | async-start | bytes 4456448 | tf_op jit(solution)/shard_map/all_gather | solution.py:80
Sparse Core Ops, SparseCore 0:
  9.2 54.5 all-gather.6
  70.3 155.6 all-gather.8
  259.0 153.0 all-reduce.10
  414.5 58.7 all-reduce.12
  476.9 91.7 all-gather.10
  581.1 152.5 all-reduce.14
  736.2 59.0 all-reduce.16
  798.9 91.7 all-gather.12
  900.5 152.4 all-reduce.18
  1055.3 58.8 all-reduce.20
  1118.3 91.7 all-gather.14
  1219.8 152.5 all-reduce.22
  1374.9 58.8 all-reduce.24
  1437.2 91.7 all-gather.16
where the time goes:
time: 1560 us; the launch traced here: 1550 us
  waiting for transfers between devices  1170 us (75%)
  other arithmetic  251 us (16%)
  local copies, waits for them, and re-layouts  69 us (4%)
  matrix products  45 us (3%)
  between operations  18.9 us (1%)
    psum x8, waiting for transfers between devices, from_root(): return lax.psum(jnp.where(mine, value, jnp.zeros_like(value)), axis)  601 us
    all_gather x4, waiting for transfers between devices, local(): complete = lax.all_gather(solved, ('row', 'col'), axis=0, tiled=True)  359 us
    all_gather x1, waiting for transfers between devices, local(): lax.all_gather(regrouped, 'row', axis=0, tiled=True)  150 us
    another operation x27, other arithmetic, local(): diag_factor = jnp.linalg.cholesky(corner)  138 us
    another operation x9, other arithmetic, solve_panel(): jax.scipy.linalg.solve_triangular(diag_factor, column_rows.T, lower=True)  78.8 us
    all_gather x1, waiting for transfers between devices, local(): gather_portion = lax.all_gather(child_updates, 'col', axis=1, tiled=True)  55.7 us
    dot_general x4, matrix products, local(): lax.dot_general(own_rows, col_rows, (((1,), (1,)), ((), ())), precision=H...  32.2 us
  transfers between devices with their start and end apart: 14, of which 10 were waited for; matrix products, arithmetic and copies ran while one was open for 17% of the time, Pallas kernels for 0%

commit v1 on v0

--- a/solution.py
+++ b/solution.py
@@ -12,7 +12,7 @@
 
 def from_root(value, axis, root):
     mine = lax.axis_index(axis) == root
-    return lax.psum(jnp.where(mine, value, jnp.zeros_like(value)), axis)
+    return jnp.sum(lax.all_gather(jnp.where(mine, value, jnp.zeros_like(value)), axis), axis=0)
 
 
 def block_select(parents, anchor, width):

time: 1560 us -> 1460 us (0.936)
  waiting for transfers between devices: 1170 us -> 1010 us
  local copies, waits for them, and re-layouts: 69 us -> 102 us
  other arithmetic: 251 us -> 271 us
    psum x8 -> x0, waiting for transfers between devices: 601 us -> none  [from_root(): return lax.psum(jnp.where(mine, value, jnp.zeros_like(value)), axis)]
    all_gather x0 -> x8, waiting for transfers between devices: none -> 489 us  [from_root(): lax.all_gather(jnp.where(mine, value, jnp.zeros_like(value)), axis)]
    all_gather x4, waiting for transfers between devices: 359 us -> 317 us  [local(): complete = lax.all_gather(solved, ('row', 'col'), axis=0, tiled=True)]
    reduce_sum x0 -> x8, other arithmetic: none -> 24.1 us  [from_root(): jnp.sum(lax.all_gather(jnp.where(mine, value, jnp.zeros_like(value)), axi...]
    all_gather x0 -> x4, local copies, waits for them, and re-layouts: none -> 24 us  [from_root(): lax.all_gather(jnp.where(mine, value, jnp.zeros_like(value)), axis)]
    unnamed x11 -> x15, local copies, waits for them, and re-layouts: 18.9 us -> 34.4 us
  transfers between devices with their start and end apart: 14 -> 14, of which waited for: 10 -> 14; matrix products, arithmetic and copies ran while one was open for 17% -> 4% of each run, Pallas kernels for 0% -> 0%
where the time goes in v1:
time: 1460 us; the launch traced here: 1450 us
  waiting for transfers between devices  1010 us (69%)
  other arithmetic  271 us (19%)
  local copies, waits for them, and re-layouts  102 us (7%)
  matrix products  45 us (3%)
  between operations  19.6 us (1%)
    all_gather x8, waiting for transfers between devices, from_root(): lax.all_gather(jnp.where(mine, value, jnp.zeros_like(value)), axis)  489 us
    all_gather x4, waiting for transfers between devices, local(): complete = lax.all_gather(solved, ('row', 'col'), axis=0, tiled=True)  317 us
    all_gather x1, waiting for transfers between devices, local(): lax.all_gather(regrouped, 'row', axis=0, tiled=True)  150 us
    another operation x27, other arithmetic, local(): diag_factor = jnp.linalg.cholesky(corner)  138 us
    another operation x9, other arithmetic, solve_panel(): jax.scipy.linalg.solve_triangular(diag_factor, column_rows.T, lower=True)  79.9 us
    all_gather x1, waiting for transfers between devices, local(): gather_portion = lax.all_gather(child_updates, 'col', axis=1, tiled=True)  55.7 us
    unnamed x15, local copies, waits for them, and re-layouts  34.4 us
    dot_general x4, matrix products, local(): lax.dot_general(own_rows, col_rows, (((1,), (1,)), ((), ())), precision=H...  32.2 us
  transfers between devices with their start and end apart: 14, of which 14 were waited for; matrix products, arithmetic and copies ran while one was open for 4% of the time, Pallas kernels for 0%

profile of v1, /device:TPU:1, one launch (start us, length us, event | category | flops | bytes accessed | tf_op | source)
XLA Modules:
  0.0 1451.6 jit_solution(13818715304982981404)
XLA Ops:
  8.1 55.7 %all-gather.23.cloned.1.call-done = bf16[1024,2048]{1,0:T(8,128)(2,1)} async-done(((bf16[1024,512]{1,0:T(8,128)(2,1)}), bf16[1024,2048]{1,0:T(8,128)(2,1)}) %all-gather.23.cloned.1.call-update) | async-done | bytes 4194320 | tf_op jit(solution)/shard_map/all_gather | solution.py:39
  75.5 150.4 %all-gather.25.cloned.1.call-done = bf16[4096,1024]{1,0:T(8,128)(2,1)} async-done(((bf16[1024,1024]{1,0:T(8,128)(2,1)}), bf16[4096,1024]{1,0:T(8,128)(2,1)}) %all-gather.25.cloned.1.call-update) | async-done | bytes 8388624 | tf_op jit(solution)/shard_map/all_gather | solution.py:58
  225.9 8.9 reshape.84
  261.2 47.8 %all-gather.37.cloned.1.call-done = f32[4096,256]{0,1:T(8,128)} async-done(((f32[1024,256]{0,1:T(8,128)}), f32[4096,256]{0,1:T(8,128)}) %all-gather.37.cloned.1.call-update) | async-done | bytes 4194320 | tf_op jit(solution)/shard_map/all_gather | solution.py:15
  319.8 74.7 %all-gather.35.cloned.1.call-done = f32[4096,256]{0,1:T(8,128)} async-done(((f32[256,256]{0,1:T(8,128)}), f32[4096,256]{0,1:T(8,128)}) %all-gather.35.cloned.1.call-update) | async-done | bytes 4194320 | tf_op jit(solution)/shard_map/all_gather | solution.py:15
  399.9 11.7 cholesky.214
  411.7 9.8 custom-call.17
  422.0 11.7 cholesky.231
  439.8 20.1 %custom-call.18 = f32[2,128,128]{1,2,0:T(8,128)S(1)} custom-call(f32[2,128,128]{2,1,0:T(8,128)S(1)} %get-tuple-element.33), custom_call_target="InvertDiagBlocksLowerTriangular" | custom-call | tf_op jit(solution)/shard_map/jit(_solve_triangular)/triangular_solve | solution.py:23
  461.7 81.2 %all-gather.27.cloned.1.call-done = f32[4096,256]{0,1:T(8,128)} async-done(((f32[256,256]{0,1:T(8,128)}), f32[4096,256]{0,1:T(8,128)}) %all-gather.27.cloned.1.call-update) | async-done | bytes 4194320 | tf_op jit(solution)/shard_map/all_gather | solution.py:80
  557.3 47.5 %all-gather.41.cloned.1.call-done = f32[4096,256]{0,1:T(8,128)} async-done(((f32[1024,256]{0,1:T(8,128)}), f32[4096,256]{0,1:T(8,128)}) %all-gather.41.cloned.1.call-update) | async-done | bytes 4194320 | tf_op jit(solution)/shard_map/all_gather | solution.py:15
  615.5 74.8 %all-gather.39.cloned.1.call-done = f32[4096,256]{0,1:T(8,128)} async-done(((f32[256,256]{0,1:T(8,128)}), f32[4096,256]{0,1:T(8,128)}) %all-gather.39.cloned.1.call-update) | async-done | bytes 4194320 | tf_op jit(solution)/shard_map/all_gather | solution.py:15
  695.7 11.7 cholesky.248
  707.5 9.8 custom-call.19
  717.8 11.7 cholesky.265
  736.4 19.9 %custom-call.20 = f32[2,128,128]{1,2,0:T(8,128)S(1)} custom-call(f32[2,128,128]{2,1,0:T(8,128)S(1)} %get-tuple-element.34), custom_call_target="InvertDiagBlocksLowerTriangular" | custom-call | tf_op jit(solution)/shard_map/jit(_solve_triangular)/triangular_solve | solution.py:23
  758.1 81.2 %all-gather.29.cloned.1.call-done = f32[4096,256]{0,1:T(8,128)} async-done(((f32[256,256]{0,1:T(8,128)}), f32[4096,256]{0,1:T(8,128)}) %all-gather.29.cloned.1.call-update) | async-done | bytes 4194320 | tf_op jit(solution)/shard_map/all_gather | solution.py:80
  851.0 47.5 %all-gather.45.cloned.1.call-done = f32[4096,256]{0,1:T(8,128)} async-done(((f32[1024,256]{0,1:T(8,128)}), f32[4096,256]{0,1:T(8,128)}) %all-gather.45.cloned.1.call-update) | async-done | bytes 4194320 | tf_op jit(solution)/shard_map/all_gather | solution.py:15
  909.3 74.7 %all-gather.43.cloned.1.call-done = f32[4096,256]{0,1:T(8,128)} async-done(((f32[256,256]{0,1:T(8,128)}), f32[4096,256]{0,1:T(8,128)}) %all-gather.43.cloned.1.call-update) | async-done | bytes 4194320 | tf_op jit(solution)/shard_map/all_gather | solution.py:15
  989.6 11.7 cholesky.282
  1001.4 9.8 custom-call.21
  1011.7 11.7 cholesky.299
  1030.0 19.8 %custom-call.22 = f32[2,128,128]{1,2,0:T(8,128)S(1)} custom-call(f32[2,128,128]{2,1,0:T(8,128)S(1)} %get-tuple-element.35), custom_call_target="InvertDiagBlocksLowerTriangular" | custom-call | tf_op jit(solution)/shard_map/jit(_solve_triangular)/triangular_solve | solution.py:23
  1051.7 81.2 %all-gather.31.cloned.1.call-done = f32[4096,256]{0,1:T(8,128)} async-done(((f32[256,256]{0,1:T(8,128)}), f32[4096,256]{0,1:T(8,128)}) %all-gather.31.cloned.1.call-update) | async-done | bytes 4194320 | tf_op jit(solution)/shard_map/all_gather | solution.py:80
  1144.6 47.5 %all-gather.49.cloned.1.call-done = f32[4096,256]{0,1:T(8,128)} async-done(((f32[1024,256]{0,1:T(8,128)}), f32[4096,256]{0,1:T(8,128)}) %all-gather.49.cloned.1.call-update) | async-done | bytes 4194320 | tf_op jit(solution)/shard_map/all_gather | solution.py:15
  1202.9 74.8 %all-gather.47.cloned.1.call-done = f32[4096,256]{0,1:T(8,128)} async-done(((f32[256,256]{0,1:T(8,128)}), f32[4096,256]{0,1:T(8,128)}) %all-gather.47.cloned.1.call-update) | async-done | bytes 4194320 | tf_op jit(solution)/shard_map/all_gather | solution.py:15
  1283.1 11.7 cholesky.316
  1294.9 9.8 custom-call.23
  1305.2 11.7 cholesky.333
  1323.5 19.9 %custom-call.24 = f32[2,128,128]{1,2,0:T(8,128)S(1)} custom-call(f32[2,128,128]{2,1,0:T(8,128)S(1)} %get-tuple-element.36), custom_call_target="InvertDiagBlocksLowerTriangular" | custom-call | tf_op jit(solution)/shard_map/jit(_solve_triangular)/triangular_solve | solution.py:23
  1353.1 73.3 %all-gather.33.cloned.1.call-done = f32[4096,256]{0,1:T(8,128)} async-done(((f32[256,256]{0,1:T(8,128)}), f32[4096,256]{0,1:T(8,128)}) %all-gather.33.cloned.1.call-update) | async-done | bytes 4194320 | tf_op jit(solution)/shard_map/all_gather | solution.py:80
  1429.1 10.2 fusion.1
  (185 shorter events, 203.7 us)
Async XLA Ops:
  6.5 57.3 %all-gather.23.cloned.1.call-start = ((), (), s32[]{:S(2)}) async-start(), calls=%async_computation | async-start | bytes 5242880 | tf_op jit(solution)/shard_map/all_gather | solution.py:39
  7.3 218.7 %all-gather.25.cloned.1.call-start = ((), (), s32[]{:S(2)}) async-start(), calls=%async_computation.1 | async-start | bytes 10485760 | tf_op jit(solution)/shard_map/all_gather | solution.py:58
  70.1 238.8 %all-gather.37.cloned.1.call-start = ((), (), s32[]{:S(2)}) async-start(), calls=%async_computation.7 | async-start | bytes 5242880 | tf_op jit(solution)/shard_map/all_gather | solution.py:15
  256.1 1.9 copy-start
  259.1 135.4 %all-gather.35.cloned.1.call-start = ((), (), s32[]{:S(2)}) async-start(), calls=%async_computation.6 | async-start | bytes 4456448 | tf_op jit(solution)/shard_map/all_gather | solution.py:15
  260.9 282.0 %all-gather.27.cloned.1.call-start = ((), (), s32[]{:S(2)}) async-start(), calls=%async_computation.2 | async-start | bytes 4456448 | tf_op jit(solution)/shard_map/all_gather | solution.py:80
  461.6 143.1 %all-gather.41.cloned.1.call-start = ((), (), s32[]{:S(2)}) async-start(), calls=%async_computation.9 | async-start | bytes 5242880 | tf_op jit(solution)/shard_map/all_gather | solution.py:15
  552.4 2.0 copy-start.1
  555.5 134.9 %all-gather.39.cloned.1.call-start = ((), (), s32[]{:S(2)}) async-start(), calls=%async_computation.8 | async-start | bytes 4456448 | tf_op jit(solution)/shard_map/all_gather | solution.py:15
  557.2 282.1 %all-gather.29.cloned.1.call-start = ((), (), s32[]{:S(2)}) async-start(), calls=%async_computation.3 | async-start | bytes 4456448 | tf_op jit(solution)/shard_map/all_gather | solution.py:80
  758.0 140.5 %all-gather.45.cloned.1.call-start = ((), (), s32[]{:S(2)}) async-start(), calls=%async_computation.11 | async-start | bytes 5242880 | tf_op jit(solution)/shard_map/all_gather | solution.py:15
  846.2 2.0 copy-start.2
  849.2 134.7 %all-gather.43.cloned.1.call-start = ((), (), s32[]{:S(2)}) async-start(), calls=%async_computation.10 | async-start | bytes 4456448 | tf_op jit(solution)/shard_map/all_gather | solution.py:15
  851.0 281.9 %all-gather.31.cloned.1.call-start = ((), (), s32[]{:S(2)}) async-start(), calls=%async_computation.4 | async-start | bytes 4456448 | tf_op jit(solution)/shard_map/all_gather | solution.py:80
  1051.6 140.5 %all-gather.49.cloned.1.call-start = ((), (), s32[]{:S(2)}) async-start(), calls=%async_computation.13 | async-start | bytes 5242880 | tf_op jit(solution)/shard_map/all_gather | solution.py:15
  1139.8 2.0 copy-start.3
  1142.8 134.9 %all-gather.47.cloned.1.call-start = ((), (), s32[]{:S(2)}) async-start(), calls=%async_computation.12 | async-start | bytes 4456448 | tf_op jit(solution)/shard_map/all_gather | solution.py:15
  1144.6 281.8 %all-gather.33.cloned.1.call-start = ((), (), s32[]{:S(2)}) async-start(), calls=%async_computation.5 | async-start | bytes 4456448 | tf_op jit(solution)/shard_map/all_gather | solution.py:80
Sparse Core Ops, SparseCore 0:
  9.2 54.5 all-gather.22
  70.3 155.6 all-gather.24
  259.2 49.7 all-gather.36
  311.2 83.1 all-gather.34
  461.7 81.0 all-gather.26
  555.6 49.0 all-gather.40
  607.1 83.1 all-gather.38
  758.1 81.1 all-gather.28
  849.4 49.0 all-gather.44
  900.7 83.1 all-gather.42
  1051.7 81.1 all-gather.30
  1143.0 49.0 all-gather.48
  1194.5 83.1 all-gather.46
  1345.2 81.1 all-gather.32
